TPU v7x, 128 devices: a whole 4x4x4 slice. The times are simulated.
128 devices in a mesh: row: 8 (over y_lo, z), col: 16 (over x, y_hi, core).
Axes of the slice: x: 4, y: 4 (y_hi: 2, y_lo: 2; y = y_hi * 2 + y_lo), z: 4, core: 2. Of those that a mesh axis runs over, the one named last changes fastest.
Arguments:
- hessian: float32 [16384, 8, 16, 128], P('row', None, 'col'), may hold values from -1 to 16, as said below
- weights: bfloat16 [512, 16384], P('col', 'row'), may hold values from -6 to 6
- codes: int32 [512, 8192], P('col', 'row'), may hold values from 0 to 255
- tile_map: int32 [32, 64], P('col', 'row'), may hold values from 0 to 511
- codebooks: float32 [512, 2, 256], replicated, may hold values from -6 to 6
Outputs:
- adjusted_codebooks: float32 [512, 2, 256], replicated
Inputs may be any that keep to these rules, and one draw needn't show every extreme that they name: `hessian`: H is symmetric with a dominant positive diagonal.
All inputs are finite; a program needn't handle non-finite values.
Results may differ from a plain program's by a relative error of at most 0.0003.
Values sent between devices are 32-bit elements; how exact they have to be, the bound alone decides.
No kernel may reach another device: no remote copies, remote signals or barrier semaphores. Data moves between devices by JAX's collectives and lax.ppermute only.
A program may use at most 64 MiB of HBM per device.

v0:
```python
import jax
import jax.numpy as jnp
from jax import lax
from jax.sharding import PartitionSpec as P

CODES = 256
NB = 512
TILE_ROWS = 16
TILE_COLS = 256
STEPS = 2
learn_rate = 0.01


def per_device(hessian, weights, codes, tile_map, codebooks):
    rows_local, cols_local = weights.shape
    rows_tiles = rows_local // TILE_ROWS
    cols_tiles = cols_local // TILE_COLS
    tile_count = rows_tiles * cols_tiles
    half_width = TILE_COLS // 2
    pair_count = TILE_ROWS * half_width
    hessian_tile = hessian.reshape(
        hessian.shape[0], hessian.shape[1] * hessian.shape[2] * hessian.shape[3]
    )
    code_tiles = (
        codes.reshape(rows_tiles, TILE_ROWS, cols_tiles, half_width)
        .transpose(0, 2, 1, 3)
        .reshape(tile_count, pair_count)
    )
    code_onehot = (
        code_tiles[:, :, None] == lax.broadcasted_iota(jnp.int32, (1, 1, CODES), 2)
    ).astype(jnp.float32)
    book_onehot = (
        tile_map.reshape(-1)[:, None] == lax.broadcasted_iota(jnp.int32, (1, NB), 1)
    ).astype(jnp.float32)
    for iteration in range(STEPS):
        tile_books = jnp.einsum(
            "tb,bck->tck", book_onehot, codebooks, precision=lax.Precision.HIGHEST
        )
        rebuilt_tiles = jnp.einsum(
            "tpk,tck->tpc", code_onehot, tile_books, precision=lax.Precision.HIGHEST
        )
        rebuilt = (
            rebuilt_tiles.reshape(rows_tiles, cols_tiles, TILE_ROWS, half_width, 2)
            .transpose(0, 2, 1, 3, 4)
            .reshape(rows_local, cols_local)
        )
        error = rebuilt - weights.astype(jnp.float32)
        gathered = lax.all_gather(error, "col", axis=0, tiled=True)
        piece_width = cols_local // lax.axis_size("col")
        error_piece = lax.dynamic_slice_in_dim(
            gathered, lax.axis_index("col") * piece_width, piece_width, 1
        )
        error_spread = lax.all_gather(error_piece, "row", axis=1, tiled=True)
        weight_grad = 2.0 * lax.psum_scatter(
            lax.dot_general(
                error_spread,
                hessian_tile,
                (((1,), (1,)), ((), ())),
                precision=lax.Precision.HIGHEST,
                preferred_element_type=jnp.float32,
            ),
            "col",
            scatter_dimension=0,
            tiled=True,
        )
        grad_tiles = (
            weight_grad.reshape(rows_tiles, TILE_ROWS, cols_tiles, half_width, 2)
            .transpose(0, 2, 1, 3, 4)
            .reshape(tile_count, pair_count, 2)
        )
        tile_grads = jnp.einsum(
            "tpk,tpc->tck", code_onehot, grad_tiles, precision=lax.Precision.HIGHEST
        )
        local_grad = jnp.einsum(
            "tb,tck->bck", book_onehot, tile_grads, precision=lax.Precision.HIGHEST
        )
        total_even, total_odd = lax.psum((local_grad[:, 0, :], local_grad[:, 1, :]), ("row", "col"))
        book_grad = jnp.stack([total_even, total_odd], axis=1)
        codebooks = codebooks - learn_rate * book_grad
    return codebooks


def solution(mesh):
    placed = (P("row", None, "col", None), P("col", "row"), P("col", "row"), P("col", "row"), P())
    return jax.shard_map(per_device, mesh=mesh, in_specs=placed, out_specs=P(), check_vma=False)
```

profile of v0, /device:TPU:1, one launch (start us, length us, event | category | flops | bytes accessed | tf_op | source)
XLA Modules:
  0.0 803.9 jit_solution(11324388309986088203)
XLA Ops:
  8.3 1.7 fusion.16
  10.0 17.1 %fusion.3 = f32[16,2048,2]{1,2,0:T(2,128)S(1)} fusion(s32[16,2048]{1,0:T(8,128)S(1)} %bitcast_bitcast_fusion, f32[16,2,256]{2,0,1:T(8,128)S(1)} %fusion.16), kind=kOutput, calls=%fused_computation.4 | convolution fusion | flops 209715200 | bytes 425984 | tf_op jit(solution)/shard_map/tpk,tck->tpc/dot_general | solution.py:39
  27.3 1.4 copy.39
  28.7 1.1 reshape.34
  31.0 59.7 %all-gather.5.cloned.1.call-done = f32[512,2048]{1,0:T(8,128)} async-done(((f32[32,2048]{1,0:T(8,128)}), f32[512,2048]{1,0:T(8,128)}) %all-gather.5.cloned.1.call-update) | async-done | bytes 4194320 | tf_op jit(solution)/shard_map/all_gather | solution.py:48
  90.7 1.7 constant_dynamic-slice_fusion.1
  92.4 39.8 %all-gather.7.cloned.1.call-done = f32[512,1024]{1,0:T(8,128)} async-done(((f32[512,128]{1,0:T(8,128)}), f32[512,1024]{1,0:T(8,128)}) %all-gather.7.cloned.1.call-update) | async-done | bytes 2097168 | tf_op jit(solution)/shard_map/all_gather | solution.py:53
  132.2 19.4 %fusion.10 = f32[512,2048]{1,0:T(8,128)} fusion(f32[512,1024]{1,0:T(8,128)} %all-gather.7.cloned.1.call-done, f32[256,8,8,128]{3,2,1,0:T(8,128)} %bitcast.51), kind=kOutput, calls=%fused_computation.11 | convolution fusion | flops 12884901888 | bytes 14680064 | tf_op jit(solution)/shard_map/dot_general | solution.py:55
  151.8 84.1 %reduce-scatter.3.cloned.1.call-done = f32[32,2048]{1,0:T(8,128)} async-done(((f32[512,2048]{1,0:T(8,128)}), f32[32,2048]{1,0:T(8,128)}) %reduce-scatter.3.cloned.1.call-update) | async-done | bytes 262160 | tf_op jit(solution)/shard_map/reduce_scatter | solution.py:54
  235.9 1.0 broadcast_multiply_fusion.1
  237.2 1.2 reshape.36
  239.4 12.3 %fusion.2 = f32[16,2,256]{2,1,0:T(2,128)S(1)} fusion(f32[16,2048,2]{1,2,0:T(2,128)S(1)} %reshape.47, s32[16,2048]{1,0:T(8,128)} %copy-done.4), kind=kOutput, calls=%fused_computation.3 | convolution fusion | flops 209715200 | bytes 425984 | tf_op jit(solution)/shard_map/tpk,tpc->tck/dot_general | solution.py:71
  252.4 1.0 fusion.38
  253.5 148.0 %all-reduce.7.cloned.1.call-done = (f32[512,1,256]{2,0,1:T(8,128)}, f32[512,1,256]{2,0,1:T(8,128)}) async-done(((f32[512,1,256]{2,0,1:T(8,128)}, f32[512,1,256]{2,0,1:T(8,128)}), (f32[512,1,256]{2,0,1:T(8,128)}, f32[512,1,256]{2,0,1:T(8,128)})) %all-reduce.7.cloned.1.call-update) | async-done | bytes 1048592 | tf_op jit(solution)/shard_map/psum | solution.py:77
  401.6 1.7 fusion.18
  403.3 17.1 %fusion.1 = f32[16,2048,2]{1,2,0:T(2,128)S(1)} fusion(s32[16,2048]{1,0:T(8,128)S(1)} %copy-done.5, f32[16,2,256]{2,0,1:T(8,128)S(1)} %fusion.18), kind=kOutput, calls=%fused_computation.2 | convolution fusion | flops 209715200 | bytes 425984 | tf_op jit(solution)/shard_map/tpk,tck->tpc/dot_general | solution.py:39
  420.6 1.4 copy.47
  422.0 2.1 reshape.39
  424.1 1.5 copy.48
  426.4 55.1 %all-gather.9.cloned.1.call-done = f32[512,2048]{1,0:T(8,128)} async-done(((f32[32,2048]{1,0:T(8,128)}), f32[512,2048]{1,0:T(8,128)}) %all-gather.9.cloned.1.call-update) | async-done | bytes 4194320 | tf_op jit(solution)/shard_map/all_gather | solution.py:48
  481.6 1.7 constant_dynamic-slice_fusion
  483.6 39.5 %all-gather.11.cloned.1.call-done = f32[512,1024]{1,0:T(8,128)} async-done(((f32[512,128]{1,0:T(8,128)}), f32[512,1024]{1,0:T(8,128)}) %all-gather.11.cloned.1.call-update) | async-done | bytes 2097168 | tf_op jit(solution)/shard_map/all_gather | solution.py:53
  523.1 19.4 %fusion.8 = f32[512,2048]{1,0:T(8,128)} fusion(f32[512,1024]{1,0:T(8,128)} %all-gather.11.cloned.1.call-done, f32[256,8,8,128]{3,2,1,0:T(8,128)} %bitcast.52), kind=kOutput, calls=%fused_computation.9 | convolution fusion | flops 12884901888 | bytes 14680064 | tf_op jit(solution)/shard_map/dot_general | solution.py:55
  542.8 84.0 %reduce-scatter.5.cloned.1.call-done = f32[32,2048]{1,0:T(8,128)} async-done(((f32[512,2048]{1,0:T(8,128)}), f32[32,2048]{1,0:T(8,128)}) %reduce-scatter.5.cloned.1.call-update) | async-done | bytes 262160 | tf_op jit(solution)/shard_map/reduce_scatter | solution.py:54
  626.9 1.0 broadcast_multiply_fusion
  627.8 1.3 copy.49
  629.2 2.5 reshape.40
  632.7 11.3 %fusion = f32[16,2,256]{2,1,0:T(2,128)S(1)} fusion(f32[16,2048,2]{1,2,0:T(2,128)S(1)} %reshape.48, s32[16,2048]{1,0:T(8,128)S(1)} %copy-done.6), kind=kOutput, calls=%fused_computation.1 | convolution fusion | flops 209715200 | bytes 425984 | tf_op jit(solution)/shard_map/tpk,tpc->tck/dot_general | solution.py:71
  644.7 1.0 fusion.37
  645.7 148.1 %all-reduce.5.cloned.1.call-done = (f32[512,1,256]{2,0,1:T(8,128)}, f32[512,1,256]{2,0,1:T(8,128)}) async-done(((f32[512,1,256]{2,0,1:T(8,128)}, f32[512,1,256]{2,0,1:T(8,128)}), (f32[512,1,256]{2,0,1:T(8,128)}, f32[512,1,256]{2,0,1:T(8,128)})) %all-reduce.5.cloned.1.call-update) | async-done | bytes 1048592 | tf_op jit(solution)/shard_map/psum | solution.py:77
  793.9 1.4 fusion.15
  795.3 1.8 copy.53
  (45 shorter events, 8.7 us)
Async XLA Ops:
  6.5 84.1 %all-gather.5.cloned.1.call-start = ((), (), s32[]{:S(2)}) async-start(), calls=%async_computation.2 | async-start | bytes 4456448 | tf_op jit(solution)/shard_map/all_gather | solution.py:48
  8.2 1.7 copy-start.4
  10.0 20.2 %copy-start.3 = (bf16[32,2048]{1,0:T(8,128)(2,1)S(1)}, bf16[32,2048]{1,0:T(8,128)(2,1)}, u32[]{:S(2)}) copy-start(bf16[32,2048]{1,0:T(8,128)(2,1)} %param.6) | copy-start | bytes 393220
  30.9 101.3 %all-gather.7.cloned.1.call-start = ((), (), s32[]{:S(2)}) async-start(), calls=%async_computation.3 | async-start | bytes 2359296 | tf_op jit(solution)/shard_map/all_gather | solution.py:53
  92.4 143.6 %reduce-scatter.3.cloned.1.call-start = ((), (), s32[]{:S(2)}) async-start(), calls=%async_computation.4 | async-start | bytes 4456448 | tf_op jit(solution)/shard_map/reduce_scatter | solution.py:54
  151.6 250.0 %all-reduce.7.cloned.1.call-start = ((), (), s32[]{:S(2)}) async-start(), calls=%async_computation.9 | async-start | bytes 2097152 | tf_op jit(solution)/shard_map/psum | solution.py:77
  239.2 162.3 %copy-start = (f32[512,2,256]{2,1,0:T(2,128)S(1)}, f32[512,2,256]{2,1,0:T(2,128)}, u32[]{:S(2)}) copy-start(f32[512,2,256]{2,1,0:T(2,128)} %param.9) | copy-start | bytes 3145732
  239.4 163.9 %copy-start.5 = (s32[16,2048]{1,0:T(8,128)S(1)}, s32[16,2048]{1,0:T(8,128)}, u32[]{:S(2)}) copy-start(s32[16,2048]{1,0:T(8,128)} %copy-done.4) | copy-start | bytes 393220
  253.5 228.1 %all-gather.9.cloned.1.call-start = ((), (), s32[]{:S(2)}) async-start(), calls=%async_computation.5 | async-start | bytes 4456448 | tf_op jit(solution)/shard_map/all_gather | solution.py:48
  426.4 96.7 %all-gather.11.cloned.1.call-start = ((), (), s32[]{:S(2)}) async-start(), calls=%async_computation.6 | async-start | bytes 2359296 | tf_op jit(solution)/shard_map/all_gather | solution.py:53
  483.3 143.6 %reduce-scatter.5.cloned.1.call-start = ((), (), s32[]{:S(2)}) async-start(), calls=%async_computation.7 | async-start | bytes 4456448 | tf_op jit(solution)/shard_map/reduce_scatter | solution.py:54
  542.5 90.2 %copy-start.6 = (s32[16,2048]{1,0:T(8,128)S(1)}, s32[16,2048]{1,0:T(8,128)}, u32[]{:S(2)}) copy-start(s32[16,2048]{1,0:T(8,128)} %copy-done.4) | copy-start | bytes 393220
  542.5 251.3 %all-reduce.5.cloned.1.call-start = ((), (), s32[]{:S(2)}) async-start(), calls=%async_computation.8 | async-start | bytes 2097152 | tf_op jit(solution)/shard_map/psum | solution.py:77
  632.5 161.4 %copy-start.1 = (f32[512,1,256]{2,0,1:T(8,128)S(1)}, f32[512,1,256]{2,0,1:T(8,128)}, u32[]{:S(2)}) copy-start(f32[512,1,256]{2,0,1:T(8,128)} %get-tuple-element.7) | copy-start | bytes 1572868
  632.5 161.4 %copy-start.2 = (f32[512,1,256]{2,0,1:T(8,128)S(1)}, f32[512,1,256]{2,0,1:T(8,128)}, u32[]{:S(2)}) copy-start(f32[512,1,256]{2,0,1:T(8,128)} %get-tuple-element.8) | copy-start | bytes 1572868
Sparse Core Ops, SparseCore 0:
  31.0 59.5 all-gather.4
  92.5 39.6 all-gather.6
  151.7 84.1 reduce-scatter.2
  253.6 147.8 all-reduce.6
  426.5 55.0 all-gather.8
  483.4 39.6 all-gather.10
  542.6 84.1 reduce-scatter.4
  645.9 147.9 all-reduce.4
where the time goes:
time: 804 us
  waiting for transfers between devices  659 us (82%)
  matrix products  101 us (13%)
  local copies, waits for them, and re-layouts  24.4 us (3%)
  between operations  13.7 us (2%)
    psum x2, waiting for transfers between devices, per_device(): lax.psum((local_grad[:, 0, :], local_grad[:, 1, :]), ('row', 'col'))  296 us
    reduce_scatter x2, waiting for transfers between devices, per_device(): lax.psum_scatter(lax.dot_general(error_spread, hessian_tile, (((1,), (1,)...  168 us
    all_gather x2, waiting for transfers between devices, per_device(): gathered = lax.all_gather(error, 'col', axis=0, tiled=True)  115 us
    all_gather x2, waiting for transfers between devices, per_device(): error_spread = lax.all_gather(error_piece, 'row', axis=1, tiled=True)  79.3 us
    dot_general x2, matrix products, per_device(): lax.dot_general(error_spread, hessian_tile, (((1,), (1,)), ((), ())), pre...  38.8 us
    dot_general x2, matrix products, per_device(): jnp.einsum('tpk,tck->tpc', code_onehot, tile_books, precision=lax.Precisi...  34.2 us
    dot_general x2, matrix products, per_device(): jnp.einsum('tpk,tpc->tck', code_onehot, grad_tiles, precision=lax.Precisi...  23.6 us
  transfers between devices with their start and end apart: 8, of which 8 were waited for; matrix products, arithmetic and copies ran while one was open for 0% of the time, Pallas kernels for 0%

commit v1 on v0

--- a/solution.py
+++ b/solution.py
@@ -74,7 +74,9 @@
         local_grad = jnp.einsum(
             "tb,tck->bck", book_onehot, tile_grads, precision=lax.Precision.HIGHEST
         )
-        total_even, total_odd = lax.psum((local_grad[:, 0, :], local_grad[:, 1, :]), ("row", "col"))
+        total_even, total_odd = lax.psum(
+            lax.psum((local_grad[:, 0, :], local_grad[:, 1, :]), "row"), "col"
+        )
         book_grad = jnp.stack([total_even, total_odd], axis=1)
         codebooks = codebooks - learn_rate * book_grad
     return codebooks

time: 804 us -> 952 us (1.18)
  waiting for transfers between devices: 659 us -> 806 us
    psum x2 -> x4, waiting for transfers between devices: 296 us -> 441 us  [the longest x2 295 us: per_device(): lax.psum(lax.psum((local_grad[:, 0, :], local_grad[:, 1, :]), 'row'), 'col')]
  transfers between devices with their start and end apart: 8 -> 10, of which waited for: 8 -> 10; matrix products, arithmetic and copies ran while one was open for 0% -> 0% of each run, Pallas kernels for 0% -> 0%
where the time goes in v1:
time: 952 us; the launch traced here: 951 us
  waiting for transfers between devices  806 us (85%)
  matrix products  101 us (11%)
  local copies, waits for them, and re-layouts  24.4 us (3%)
  between operations  13.7 us (1%)
    psum x2, waiting for transfers between devices, per_device(): lax.psum(lax.psum((local_grad[:, 0, :], local_grad[:, 1, :]), 'row'), 'col')  295 us
    reduce_scatter x2, waiting for transfers between devices, per_device(): lax.psum_scatter(lax.dot_general(error_spread, hessian_tile, (((1,), (1,)...  168 us
    psum x2, waiting for transfers between devices, per_device(): lax.psum((local_grad[:, 0, :], local_grad[:, 1, :]), 'row')  146 us
    all_gather x2, waiting for transfers between devices, per_device(): gathered = lax.all_gather(error, 'col', axis=0, tiled=True)  117 us
    all_gather x2, waiting for transfers between devices, per_device(): error_spread = lax.all_gather(error_piece, 'row', axis=1, tiled=True)  79.3 us
    dot_general x2, matrix products, per_device(): lax.dot_general(error_spread, hessian_tile, (((1,), (1,)), ((), ())), pre...  38.8 us
    dot_general x2, matrix products, per_device(): jnp.einsum('tpk,tck->tpc', code_onehot, tile_books, precision=lax.Precisi...  34.2 us
    dot_general x2, matrix products, per_device(): jnp.einsum('tpk,tpc->tck', code_onehot, grad_tiles, precision=lax.Precisi...  23.6 us
  transfers between devices with their start and end apart: 10, of which 10 were waited for; matrix products, arithmetic and copies ran while one was open for 0% of the time, Pallas kernels for 0%

profile of v1, /device:TPU:1, one launch (start us, length us, event | category | flops | bytes accessed | tf_op | source)
XLA Modules:
  0.0 951.2 jit_solution(15843067211565523985)
XLA Ops:
  8.3 1.7 fusion.16
  10.0 17.1 %fusion.3 = f32[16,2048,2]{1,2,0:T(2,128)S(1)} fusion(s32[16,2048]{1,0:T(8,128)S(1)} %bitcast_bitcast_fusion, f32[16,2,256]{2,0,1:T(8,128)S(1)} %fusion.16), kind=kOutput, calls=%fused_computation.4 | convolution fusion | flops 209715200 | bytes 425984 | tf_op jit(solution)/shard_map/tpk,tck->tpc/dot_general | solution.py:39
  27.3 1.4 copy.39
  28.7 1.1 reshape.34
  31.0 59.7 %all-gather.5.cloned.1.call-done = f32[512,2048]{1,0:T(8,128)} async-done(((f32[32,2048]{1,0:T(8,128)}), f32[512,2048]{1,0:T(8,128)}) %all-gather.5.cloned.1.call-update) | async-done | bytes 4194320 | tf_op jit(solution)/shard_map/all_gather | solution.py:48
  90.7 1.7 constant_dynamic-slice_fusion.1
  92.4 39.8 %all-gather.7.cloned.1.call-done = f32[512,1024]{1,0:T(8,128)} async-done(((f32[512,128]{1,0:T(8,128)}), f32[512,1024]{1,0:T(8,128)}) %all-gather.7.cloned.1.call-update) | async-done | bytes 2097168 | tf_op jit(solution)/shard_map/all_gather | solution.py:53
  132.2 19.4 %fusion.10 = f32[512,2048]{1,0:T(8,128)} fusion(f32[512,1024]{1,0:T(8,128)} %all-gather.7.cloned.1.call-done, f32[256,8,8,128]{3,2,1,0:T(8,128)} %bitcast.63), kind=kOutput, calls=%fused_computation.11 | convolution fusion | flops 12884901888 | bytes 14680064 | tf_op jit(solution)/shard_map/dot_general | solution.py:55
  151.8 84.1 %reduce-scatter.3.cloned.1.call-done = f32[32,2048]{1,0:T(8,128)} async-done(((f32[512,2048]{1,0:T(8,128)}), f32[32,2048]{1,0:T(8,128)}) %reduce-scatter.3.cloned.1.call-update) | async-done | bytes 262160 | tf_op jit(solution)/shard_map/reduce_scatter | solution.py:54
  237.2 1.2 reshape.36
  239.4 12.3 %fusion.2 = f32[16,2,256]{2,1,0:T(2,128)S(1)} fusion(f32[16,2048,2]{1,2,0:T(2,128)S(1)} %reshape.43, s32[16,2048]{1,0:T(8,128)} %copy-done.4), kind=kOutput, calls=%fused_computation.3 | convolution fusion | flops 209715200 | bytes 425984 | tf_op jit(solution)/shard_map/tpk,tpc->tck/dot_general | solution.py:71
  252.4 1.0 slice_bitcast_fusion.3
  253.5 72.9 %all-reduce.15.cloned.1.call-done = (f32[512,256]{1,0:T(8,128)}, f32[512,256]{1,0:T(8,128)}) async-done(((f32[512,256]{1,0:T(8,128)}, f32[512,256]{1,0:T(8,128)}), (f32[512,256]{1,0:T(8,128)}, f32[512,256]{1,0:T(8,128)})) %all-reduce.15.cloned.1.call-update) | async-done | bytes 1048592 | tf_op jit(solution)/shard_map/psum | solution.py:78
  326.6 147.4 %all-reduce.11.cloned.1.call-done = (f32[512,1,256]{2,0,1:T(8,128)}, f32[512,1,256]{2,0,1:T(8,128)}) async-done(((f32[512,1,256]{2,0,1:T(8,128)}, f32[512,1,256]{2,0,1:T(8,128)}), (f32[512,1,256]{2,0,1:T(8,128)}, f32[512,1,256]{2,0,1:T(8,128)})) %all-reduce.11.cloned.1.call-update) | async-done | bytes 1048592 | tf_op jit(solution)/shard_map/psum | solution.py:77
  474.0 1.7 fusion.18
  475.7 17.1 %fusion.1 = f32[16,2048,2]{1,2,0:T(2,128)S(1)} fusion(s32[16,2048]{1,0:T(8,128)S(1)} %copy-done.5, f32[16,2,256]{2,0,1:T(8,128)S(1)} %fusion.18), kind=kOutput, calls=%fused_computation.2 | convolution fusion | flops 209715200 | bytes 425984 | tf_op jit(solution)/shard_map/tpk,tck->tpc/dot_general | solution.py:39
  493.1 1.4 copy.47
  494.4 2.1 reshape.39
  496.5 1.5 copy.48
  498.9 57.7 %all-gather.9.cloned.1.call-done = f32[512,2048]{1,0:T(8,128)} async-done(((f32[32,2048]{1,0:T(8,128)}), f32[512,2048]{1,0:T(8,128)}) %all-gather.9.cloned.1.call-update) | async-done | bytes 4194320 | tf_op jit(solution)/shard_map/all_gather | solution.py:48
  556.6 1.7 constant_dynamic-slice_fusion
  558.6 39.5 %all-gather.11.cloned.1.call-done = f32[512,1024]{1,0:T(8,128)} async-done(((f32[512,128]{1,0:T(8,128)}), f32[512,1024]{1,0:T(8,128)}) %all-gather.11.cloned.1.call-update) | async-done | bytes 2097168 | tf_op jit(solution)/shard_map/all_gather | solution.py:53
  598.1 19.4 %fusion.8 = f32[512,2048]{1,0:T(8,128)} fusion(f32[512,1024]{1,0:T(8,128)} %all-gather.11.cloned.1.call-done, f32[256,8,8,128]{3,2,1,0:T(8,128)} %bitcast.64), kind=kOutput, calls=%fused_computation.9 | convolution fusion | flops 12884901888 | bytes 14680064 | tf_op jit(solution)/shard_map/dot_general | solution.py:55
  617.6 84.3 %reduce-scatter.5.cloned.1.call-done = f32[32,2048]{1,0:T(8,128)} async-done(((f32[512,2048]{1,0:T(8,128)}), f32[32,2048]{1,0:T(8,128)}) %reduce-scatter.5.cloned.1.call-update) | async-done | bytes 262160 | tf_op jit(solution)/shard_map/reduce_scatter | solution.py:54
  702.8 1.3 copy.49
  704.2 2.5 reshape.40
  707.7 11.3 %fusion = f32[16,2,256]{2,1,0:T(2,128)S(1)} fusion(f32[16,2048,2]{1,2,0:T(2,128)S(1)} %reshape.44, s32[16,2048]{1,0:T(8,128)S(1)} %copy-done.6), kind=kOutput, calls=%fused_computation.1 | convolution fusion | flops 209715200 | bytes 425984 | tf_op jit(solution)/shard_map/tpk,tpc->tck/dot_general | solution.py:71
  719.7 1.0 slice_bitcast_fusion.1
  720.8 72.9 %all-reduce.13.cloned.1.call-done = (f32[512,256]{1,0:T(8,128)}, f32[512,256]{1,0:T(8,128)}) async-done(((f32[512,256]{1,0:T(8,128)}, f32[512,256]{1,0:T(8,128)}), (f32[512,256]{1,0:T(8,128)}, f32[512,256]{1,0:T(8,128)})) %all-reduce.13.cloned.1.call-update) | async-done | bytes 1048592 | tf_op jit(solution)/shard_map/psum | solution.py:78
  793.7 147.5 %all-reduce.9.cloned.1.call-done = (f32[512,1,256]{2,0,1:T(8,128)}, f32[512,1,256]{2,0,1:T(8,128)}) async-done(((f32[512,1,256]{2,0,1:T(8,128)}, f32[512,1,256]{2,0,1:T(8,128)}), (f32[512,1,256]{2,0,1:T(8,128)}, f32[512,1,256]{2,0,1:T(8,128)})) %all-reduce.9.cloned.1.call-update) | async-done | bytes 1048592 | tf_op jit(solution)/shard_map/psum | solution.py:77
  941.2 1.4 fusion.15
  942.6 1.8 copy.53
  (51 shorter events, 10.4 us)
Async XLA Ops:
  6.5 84.1 %all-gather.5.cloned.1.call-start = ((), (), s32[]{:S(2)}) async-start(), calls=%async_computation.2 | async-start | bytes 4456448 | tf_op jit(solution)/shard_map/all_gather | solution.py:48
  8.2 1.7 copy-start.4
  10.0 20.2 %copy-start.3 = (bf16[32,2048]{1,0:T(8,128)(2,1)S(1)}, bf16[32,2048]{1,0:T(8,128)(2,1)}, u32[]{:S(2)}) copy-start(bf16[32,2048]{1,0:T(8,128)(2,1)} %param.6) | copy-start | bytes 393220
  30.9 101.3 %all-gather.7.cloned.1.call-start = ((), (), s32[]{:S(2)}) async-start(), calls=%async_computation.3 | async-start | bytes 2359296 | tf_op jit(solution)/shard_map/all_gather | solution.py:53
  92.4 143.6 %reduce-scatter.3.cloned.1.call-start = ((), (), s32[]{:S(2)}) async-start(), calls=%async_computation.4 | async-start | bytes 4456448 | tf_op jit(solution)/shard_map/reduce_scatter | solution.py:54
  151.6 174.9 %all-reduce.15.cloned.1.call-start = ((), (), s32[]{:S(2)}) async-start(), calls=%async_computation.11 | async-start | bytes 2097152 | tf_op jit(solution)/shard_map/psum | solution.py:78
  239.2 234.7 %copy-start = (f32[512,2,256]{2,1,0:T(2,128)S(1)}, f32[512,2,256]{2,1,0:T(2,128)}, u32[]{:S(2)}) copy-start(f32[512,2,256]{2,1,0:T(2,128)} %param.9) | copy-start | bytes 3145732
  239.4 236.3 %copy-start.5 = (s32[16,2048]{1,0:T(8,128)S(1)}, s32[16,2048]{1,0:T(8,128)}, u32[]{:S(2)}) copy-start(s32[16,2048]{1,0:T(8,128)} %copy-done.4) | copy-start | bytes 393220
  253.5 220.5 %all-reduce.11.cloned.1.call-start = ((), (), s32[]{:S(2)}) async-start(), calls=%async_computation.9 | async-start | bytes 2097152 | tf_op jit(solution)/shard_map/psum | solution.py:77
  326.5 230.1 %all-gather.9.cloned.1.call-start = ((), (), s32[]{:S(2)}) async-start(), calls=%async_computation.5 | async-start | bytes 4456448 | tf_op jit(solution)/shard_map/all_gather | solution.py:48
  498.8 99.3 %all-gather.11.cloned.1.call-start = ((), (), s32[]{:S(2)}) async-start(), calls=%async_computation.6 | async-start | bytes 2359296 | tf_op jit(solution)/shard_map/all_gather | solution.py:53
  558.3 143.6 %reduce-scatter.5.cloned.1.call-start = ((), (), s32[]{:S(2)}) async-start(), calls=%async_computation.7 | async-start | bytes 4456448 | tf_op jit(solution)/shard_map/reduce_scatter | solution.py:54
  617.5 90.2 %copy-start.6 = (s32[16,2048]{1,0:T(8,128)S(1)}, s32[16,2048]{1,0:T(8,128)}, u32[]{:S(2)}) copy-start(s32[16,2048]{1,0:T(8,128)} %copy-done.4) | copy-start | bytes 393220
  617.5 176.1 %all-reduce.13.cloned.1.call-start = ((), (), s32[]{:S(2)}) async-start(), calls=%async_computation.10 | async-start | bytes 2097152 | tf_op jit(solution)/shard_map/psum | solution.py:78
  707.5 233.7 %copy-start.1 = (f32[512,1,256]{2,0,1:T(8,128)S(1)}, f32[512,1,256]{2,0,1:T(8,128)}, u32[]{:S(2)}) copy-start(f32[512,1,256]{2,0,1:T(8,128)} %get-tuple-element.7) | copy-start | bytes 1572868
  707.5 233.7 %copy-start.2 = (f32[512,1,256]{2,0,1:T(8,128)S(1)}, f32[512,1,256]{2,0,1:T(8,128)}, u32[]{:S(2)}) copy-start(f32[512,1,256]{2,0,1:T(8,128)} %get-tuple-element.8) | copy-start | bytes 1572868
  720.8 220.4 %all-reduce.9.cloned.1.call-start = ((), (), s32[]{:S(2)}) async-start(), calls=%async_computation.8 | async-start | bytes 2097152 | tf_op jit(solution)/shard_map/psum | solution.py:77
Sparse Core Ops, SparseCore 0:
  31.0 59.5 all-gather.4
  92.5 39.6 all-gather.6
  151.7 84.1 reduce-scatter.2
  253.6 72.8 all-reduce.14
  329.0 144.9 all-reduce.10
  499.0 57.5 all-gather.8
  558.4 39.6 all-gather.10
  617.6 84.1 reduce-scatter.4
  720.9 72.7 all-reduce.12
  796.2 144.9 all-reduce.8
